TPU v7x, 128 devices: a whole 4x4x4 slice. The times are simulated.
128 devices in a mesh: seq: 16 (over y, x), mp: 8 (over z, core).
Axes of the slice: x: 4, y: 4, z: 4, core: 2. Of those that a mesh axis runs over, the one named last changes fastest.
Arguments:
- residual_activations: bfloat16 [16384, 4096], P('seq', 'mp'), may hold values from -6 to 6
- prelayer_gain_vector: bfloat16 [4096], replicated, may hold values from 0.099609375 to 1.8984375
- gating_projection: bfloat16 [4096], replicated, may hold values from -0.25 to 0.25
- asker_projection: bfloat16 [4096, 8192], P(None, 'mp'), may hold values from -0.09375 to 0.09375
- lookup_projection: bfloat16 [4096, 1024], P(None, 'mp'), may hold values from -0.09375 to 0.09375
- content_projection: bfloat16 [4096, 1024], P(None, 'mp'), may hold values from -0.09375 to 0.09375
- final_projection: bfloat16 [8192, 4096], P(None, 'mp'), may hold values from -0.0625 to 0.0625
- logit_sharpness: float32 [64], P('mp'), may hold values from 1 to 64
- selection_table: int32 [16, 256], P('seq'), may hold values from 0 to 1023, as said below
- dispatched_tally_table: int32 [16, 16], replicated, may hold values from 0 to 16, as said below
Outputs:
- blended: bfloat16 [16384, 4096], P('seq', 'mp')
Inputs may be any that keep to these rules, and one draw needn't show every extreme that they name: `dispatched_tally_table`: entry [s, d] counts the routed tokens of source shard s whose compacted place falls to owner d: the compacted sequence lists all routed tokens in sequence order and is dealt in blocks of 8 places, block b to owner b mod 16. Every entry is a multiple of 8, and every column sums to 128. `selection_table`: row s lists in increasing order the distinct local indices of the routed tokens of source shard s, as many as row s of dispatched_tally_table sums to, and zeros after them.
All inputs are finite; a program needn't handle non-finite values.
Results may differ from a plain program's by a relative error of at most 0.0059.
Values may be sent and summed in bfloat16 or wider, within the bound.
No kernel may reach another device: no remote copies, remote signals or barrier semaphores. Data moves between devices by JAX's collectives and lax.ppermute only.
A program may use at most 64 MiB of HBM per device.

v0:
```python
import math
import jax
import jax.numpy as jnp
from jax import lax
from jax.sharding import PartitionSpec as P

HEADS = 64
SHARED_KV_COUNT = 8
PER_HEAD_DIM = 128
SEL = 128


def compact(incoming, prefix, spans, shard, nseq, owned):
    span_ids = jnp.arange(nseq, dtype=jnp.int32) * nseq + shard
    source_of = jnp.sum(
        (prefix[None, :] + spans[None, :] <= span_ids[:, None]).astype(jnp.int32), axis=1
    )
    matches = source_of[:, None] == jnp.arange(nseq, dtype=jnp.int32)[None, :]
    start_of = jnp.sum(jnp.where(matches, prefix[None, :], 0), axis=1)
    half_of = (span_ids - start_of) // nseq
    blocks = incoming.reshape(2 * nseq, incoming.shape[2], incoming.shape[3])
    return blocks[half_of * nseq + source_of].reshape(owned, incoming.shape[3])


def build_return(delta, prefix, spans, shard, nseq, block_rows):
    first = (shard - prefix) % nseq
    counter = jnp.arange(2, dtype=jnp.int32)[:, None] * nseq + first[None, :]
    usable = counter < spans[None, :]
    target = jnp.minimum((prefix[None, :] + counter) // nseq, nseq - 1)
    blocks = delta.reshape(nseq, block_rows, delta.shape[1])[target]
    return jnp.where(usable[:, :, None, None], blocks, jnp.zeros_like(blocks))


def on_device(
    residual_activations,
    prelayer_gain_vector,
    gating_projection,
    asker_projection,
    lookup_projection,
    content_projection,
    final_projection,
    logit_sharpness,
    selection_table,
    dispatched_tally_table,
):
    nseq = lax.axis_size("seq")
    shard = lax.axis_index("seq")
    owned = SEL
    block_rows = owned // nseq
    slots = selection_table.shape[1]
    sent = jnp.sum(dispatched_tally_table, axis=1)
    spans = sent // block_rows
    prefix = jnp.cumsum(spans) - spans
    mine = jnp.arange(nseq, dtype=jnp.int32) == shard
    my_prefix = jnp.sum(jnp.where(mine, prefix, 0))
    my_sent = jnp.sum(jnp.where(mine, sent, 0))
    rotation = my_prefix % nseq
    index_list = selection_table[0]
    live = jnp.arange(slots) < my_sent
    gathered_rows = residual_activations[index_list]
    gathered_rows = jnp.where(live[:, None], gathered_rows, jnp.zeros_like(gathered_rows))
    whole_rows = lax.all_gather(gathered_rows, "mp", axis=1, tiled=True)
    outgoing = jnp.roll(
        whole_rows.reshape(2, nseq, block_rows, whole_rows.shape[1]), rotation, axis=1
    )
    incoming = lax.all_to_all(outgoing, "seq", split_axis=1, concat_axis=1, tiled=True)
    full = compact(incoming, prefix, spans, shard, nseq, owned)
    gate = jax.nn.sigmoid(jnp.dot(full, gating_projection, preferred_element_type=jnp.float32))
    widened = full.astype(jnp.float32)
    inverse = lax.rsqrt(jnp.mean(widened * widened, axis=1, keepdims=True) + 1e-05)
    normed = (widened * inverse * prelayer_gain_vector.astype(jnp.float32)).astype(jnp.bfloat16)
    query = jnp.dot(normed, asker_projection, preferred_element_type=jnp.float32).astype(
        jnp.bfloat16
    )
    keys = jnp.dot(normed, lookup_projection, preferred_element_type=jnp.float32).astype(
        jnp.bfloat16
    )
    values = jnp.dot(normed, content_projection, preferred_element_type=jnp.float32).astype(
        jnp.bfloat16
    )
    paired = jnp.stack([keys, values])
    memory_pair_portion = lookup_projection.shape[1] // PER_HEAD_DIM
    asker_cluster = HEADS // SHARED_KV_COUNT
    query_heads = query.reshape(owned, memory_pair_portion, asker_cluster, PER_HEAD_DIM)
    gating_multipliers = logit_sharpness.reshape(memory_pair_portion, asker_cluster) / math.sqrt(
        PER_HEAD_DIM
    )
    own_slots = jnp.arange(owned, dtype=jnp.int32)
    query_places = (
        own_slots // block_rows * nseq * block_rows + shard * block_rows + own_slots % block_rows
    )
    start_best = jnp.full((memory_pair_portion, asker_cluster, owned), -1e30, jnp.float32)
    piece = lax.all_gather(paired, "seq", axis=1, tiled=True)
    best = start_best
    count = piece.shape[1]
    key_piece = piece[0].reshape(count, memory_pair_portion, PER_HEAD_DIM)
    value_piece = piece[1].reshape(count, memory_pair_portion, PER_HEAD_DIM)
    index_all = jnp.arange(count, dtype=jnp.int32)
    owner = index_all // owned
    position = index_all % owned
    key_places = (
        position // block_rows * nseq * block_rows + owner * block_rows + position % block_rows
    )
    allowed = key_places[None, :] <= query_places[:, None]
    score = jnp.einsum("qngd,knd->ngqk", query_heads, key_piece, preferred_element_type=jnp.float32)
    score = jnp.where(allowed[None, None], score * gating_multipliers[:, :, None, None], -1e30)
    new_best = jnp.maximum(best, jnp.max(score, axis=3))
    weights = jnp.where(allowed[None, None], jnp.exp(score - new_best[..., None]), 0.0)
    totals = jnp.sum(weights, axis=3)
    mixed = jnp.einsum(
        "ngqk,knd->ngqd",
        weights.astype(jnp.bfloat16),
        value_piece,
        preferred_element_type=jnp.float32,
    )
    sums = mixed
    best, totals, sums = (new_best, totals, sums)
    attended = (sums / totals[..., None]).astype(jnp.bfloat16)
    attended = attended.transpose(2, 0, 1, 3).reshape(
        owned, memory_pair_portion * asker_cluster * PER_HEAD_DIM
    )
    projected = jnp.dot(
        lax.all_gather(attended, "mp", axis=1, tiled=True),
        final_projection,
        preferred_element_type=jnp.float32,
    )
    delta = (gate[:, None] * projected).astype(jnp.bfloat16)
    outgoing_back = build_return(delta, prefix, spans, shard, nseq, block_rows)
    coming_back = lax.all_to_all(outgoing_back, "seq", split_axis=1, concat_axis=1, tiled=True)
    restored = jnp.roll(coming_back, -rotation, axis=1).reshape(slots, delta.shape[1])
    restored = jnp.where(live[:, None], restored, jnp.zeros_like(restored))
    updated = (
        residual_activations.astype(jnp.float32).at[index_list].add(restored.astype(jnp.float32))
    )
    return updated.astype(jnp.bfloat16)


def solution(mesh):
    placed = (
        P("seq", "mp"),
        P(),
        P(),
        P(None, "mp"),
        P(None, "mp"),
        P(None, "mp"),
        P(None, "mp"),
        P("mp"),
        P("seq", None),
        P(),
    )
    return jax.shard_map(
        on_device, mesh=mesh, in_specs=placed, out_specs=P("seq", "mp"), check_vma=False
    )
```

profile of v0, /device:TPU:1, one launch (start us, length us, event | category | flops | bytes accessed | tf_op | source)
XLA Modules:
  0.0 201.7 jit_solution(617594323271170253)
XLA Ops:
  6.5 0.9 reduce_sum.69
  7.7 0.6 and_select_fusion.4
  8.3 0.6 iota_compare_fusion.1
  9.0 0.7 compare_select_fusion
  9.7 2.6 %gather_fusion = bf16[256,512]{1,0:T(8,128)(2,1)S(1)} fusion(bf16[1024,512]{1,0:T(8,128)(2,1)} %param.10, s32[1024]{0:T(1024)S(1)} %pad_clamp_fusion.2), kind=kCustom, calls=%fused_computation | custom fusion | bytes 525312 | tf_op jit(solution)/shard_map/gather | solution.py:60
  12.3 0.8 broadcast_select_fusion
  13.1 0.6 fusion.52
  15.6 26.6 %all-gather.4.cloned.1.call-done = bf16[256,4096]{1,0:T(8,128)(2,1)} async-done(((bf16[256,512]{1,0:T(8,128)(2,1)}), bf16[256,4096]{1,0:T(8,128)(2,1)}) %all-gather.4.cloned.1.call-update) | async-done | bytes 2097168 | tf_op jit(solution)/shard_map/all_gather | solution.py:62
  42.3 2.4 %fusion.7 = bf16[2,16,8,4096]{3,2,1,0:T(8,128)(2,1)S(1)} fusion(s32[]{:T(128)S(6)} %select_n.208, bf16[2,16,8,4096]{3,2,1,0:T(8,128)(2,1)} %bitcast.124), kind=kLoop, calls=%fused_computation.15 | loop fusion | flops 1048576 | bytes 4194308 | tf_op jit(solution)/shard_map/jit(_roll_dynamic)/concatenate | solution.py:63
  44.6 1.5 copy.48
  46.1 6.6 %all-to-all-start = ((bf16[2,16,8,4096]{3,2,0,1:T(8,128)(2,1)}), bf16[2,16,8,4096]{3,2,0,1:T(8,128)(2,1)S(1)}, u32[]{:S(2)}, u32[]{:S(2)}) async-start(bf16[2,16,8,4096]{3,2,0,1:T(8,128)(2,1)} %copy.48), calls=%async_computation | async-start | bytes 4194304 | tf_op jit(solution)/shard_map/all_to_all | solution.py:66
  53.2 32.2 %all-to-all-done = bf16[2,16,8,4096]{3,2,0,1:T(8,128)(2,1)S(1)} async-done(((bf16[2,16,8,4096]{3,2,0,1:T(8,128)(2,1)}), bf16[2,16,8,4096]{3,2,0,1:T(8,128)(2,1)S(1)}, u32[]{:S(2)}, u32[]{:S(2)}) %all-to-all-start) | async-done | bytes 2097184 | tf_op jit(solution)/shard_map/all_to_all | solution.py:66
  85.4 1.5 copy.38
  86.9 2.2 %gather_fusion.1 = bf16[16,8,4096]{2,1,0:T(8,128)(2,1)S(1)} fusion(bf16[32,8,4096]{2,1,0:T(8,128)(2,1)} %bitcast.123, s32[1024]{0:T(1024)S(1)} %pad_clamp_fusion.1), kind=kCustom, calls=%fused_computation.1 | custom fusion | bytes 2097216 | tf_op jit(solution)/shard_map/gather | solution.py:22
  89.5 0.5 fusion.11
  90.0 1.7 fusion.12
  91.8 0.6 pad_maximum_fusion
  92.9 4.7 %fusion.8 = bf16[16,8,8,128]{3,2,1,0:T(8,128)(2,1)S(1)} fusion(bf16[4096,1024]{1,0:T(8,128)(2,1)} %param.13, bf16[16,8,4096]{2,1,0:T(8,128)(2,1)S(1)} %gather_fusion.1, f32[4096]{0:T(1024)S(1)} %convert_element_type.49, f32[128]{0:T(128)S(1)} %rsqrt.12), kind=kOutput, calls=%fused_computation.20 | convolution fusion | flops 1075970048 | bytes 9716224 | tf_op jit(solution)/shard_map/dot_general | solution.py:72
  97.6 34.0 %all-gather.6.cloned.1.call-done = bf16[2,2048,128]{2,1,0:T(8,128)(2,1)} async-done(((bf16[2,128,128]{2,1,0:T(8,128)(2,1)}), bf16[2,2048,128]{2,1,0:T(8,128)(2,1)}) %all-gather.6.cloned.1.call-update) | async-done | bytes 1048592 | tf_op jit(solution)/shard_map/all_gather | solution.py:93
  131.6 2.3 %fusion = (f32[8,128]{1,0:T(8,128)S(1)}, f32[2048,128,8]{1,0,2:T(8,128)S(1)}) fusion(f32[8]{0:T(128)S(1)} %broadcast_multiply_fusion, pred[128,2048]{0,1:T(8,128)(4,1)S(1)} %broadcast_compare_fusion, bf16[16,8,8,128]{3,2,1,0:T(8,128)(2,1)S(1)} %fusion.8, bf16[2,2048,128]{2,1,0:T(8,128)(2,1)} %all-gather.6.cloned.1.call-done), kind=kOutput, calls=%fused_computation.7 | convolution fusion | flops 543161344 | bytes 9441312 | tf_op jit(solution)/shard_map/qngd,knd->ngqk/dot_general | solution.py:105
  133.9 2.1 %fusion.1 = f32[8,128]{1,0:T(8,128)S(1)} fusion(f32[2048,128,8]{1,0,2:T(8,128)S(1)} %get-tuple-element.10, f32[8,128]{1,0:T(8,128)S(1)} %broadcast_maximum_fusion, f32[8]{0:T(128)S(1)} %broadcast_multiply_fusion, pred[128,2048]{0,1:T(8,128)(4,1)S(1)} %broadcast_compare_fusion), kind=kLoop, calls=%fused_computation.8 | loop fusion | flops 10484736 | bytes 8658976 | tf_op jit(solution)/shard_map/reduce_sum | solution.py:109
  136.0 2.8 %fusion.21 = bf16[8,128,128]{1,2,0:T(8,128)(2,1)} fusion(f32[2048,128,8]{1,0,2:T(8,128)S(1)} %get-tuple-element.10, f32[8,128]{1,0:T(8,128)S(1)} %broadcast_maximum_fusion, f32[8]{0:T(128)S(1)} %broadcast_multiply_fusion, pred[128,2048]{0,1:T(8,128)(4,1)S(1)} %broadcast_compare_fusion, bf16[2,2048,128]{2,1,0:T(8,128)(2,1)S(1)} %copy-done.2, ...), kind=kOutput, calls=%fused_computation.34 | convolution fusion | flops 547618816 | bytes 9445888 | tf_op jit(solution)/shard_map/ngqk,knd->ngqd/dot_general | solution.py:110
  139.2 0.4 fusion.16
  139.5 26.0 %all-gather.8.cloned.1.call-done = bf16[128,8192]{0,1:T(8,128)(2,1)} async-done(((bf16[128,1024]{0,1:T(8,128)(2,1)}), bf16[128,8192]{0,1:T(8,128)(2,1)}) %all-gather.8.cloned.1.call-update) | async-done | bytes 2097168 | tf_op jit(solution)/shard_map/all_gather | solution.py:123
  165.5 5.3 %fusion.10 = bf16[16,8,512]{2,1,0:T(8,128)(2,1)S(1)} fusion(bf16[128,8192]{0,1:T(8,128)(2,1)} %all-gather.8.cloned.1.call-done, bf16[8192,512]{1,0:T(8,128)(2,1)} %param.16, f32[128]{0:T(128)S(1)} %fusion.16), kind=kOutput, calls=%fused_computation.22 | convolution fusion | flops 1073872896 | bytes 10617344 | tf_op jit(solution)/shard_map/dot_general | solution.py:122
  170.9 0.6 gather_fusion.2
  171.5 0.7 copy.42
  172.3 6.5 %all-to-all-start.1 = ((bf16[2,16,8,512]{3,2,0,1:T(8,128)(2,1)}), bf16[2,16,8,512]{3,2,0,1:T(8,128)(2,1)S(1)}, u32[]{:S(2)}, u32[]{:S(2)}) async-start(bf16[2,16,8,512]{3,2,0,1:T(8,128)(2,1)} %copy.42), calls=%async_computation.1 | async-start | bytes 524288 | tf_op jit(solution)/shard_map/all_to_all | solution.py:129
  178.8 1.6 convert_element_type.45
  180.5 6.6 %all-to-all-done.1 = bf16[2,16,8,512]{3,2,0,1:T(8,128)(2,1)S(1)} async-done(((bf16[2,16,8,512]{3,2,0,1:T(8,128)(2,1)}), bf16[2,16,8,512]{3,2,0,1:T(8,128)(2,1)S(1)}, u32[]{:S(2)}, u32[]{:S(2)}) %all-to-all-start.1) | async-done | bytes 262176 | tf_op jit(solution)/shard_map/all_to_all | solution.py:129
  187.3 5.2 %scatter_custom_fusion = f32[1024,512]{1,0:T(8,128)} fusion(f32[1024,512]{1,0:T(8,128)} %convert_element_type.45, s32[256]{0:T(256)S(1)} %bitcast.128, bf16[256,512]{1,0:T(8,128)(2,1)S(1)} %bitcast_select_fusion.1), kind=kCustom, calls=%fused_computation.40 | custom fusion | flops 262144 | bytes 2359296 | tf_op jit(solution)/shard_map/scatter-add | solution.py:133
  192.5 2.7 %convert_element_type.59 = bf16[1024,512]{1,0:T(8,128)(2,1)} convert(f32[1024,512]{1,0:T(8,128)} %scatter_custom_fusion) | non-fusion elementwise | flops 524288 | bytes 3145728 | tf_op jit(solution)/shard_map/convert_element_type | solution.py:135
  (46 shorter events, 2.2 us)
Async XLA Ops:
  6.5 82.9 %copy-start = (bf16[4096,128]{1,0:T(8,128)(2,1)S(1)}, bf16[4096,128]{1,0:T(8,128)(2,1)}, u32[]{:S(2)}) copy-start(bf16[4096,128]{1,0:T(8,128)(2,1)} %param.14) | copy-start | bytes 3145732
  6.5 35.7 %all-gather.4.cloned.1.call-start = ((), (), s32[]{:S(2)}) async-start(), calls=%async_computation.2 | async-start | bytes 2359296 | tf_op jit(solution)/shard_map/all_gather | solution.py:62
  46.1 6.7 %copy-start.3 = (bf16[4096]{0:T(1024)(128)(2,1)S(1)}, bf16[4096]{0:T(1024)(128)(2,1)}, u32[]{:S(2)}) copy-start(bf16[4096]{0:T(1024)(128)(2,1)} %param.11) | copy-start | bytes 24580
  46.1 39.3 %all-to-all-start = ((bf16[2,16,8,4096]{3,2,0,1:T(8,128)(2,1)}), bf16[2,16,8,4096]{3,2,0,1:T(8,128)(2,1)S(1)}, u32[]{:S(2)}, u32[]{:S(2)}) async-start(bf16[2,16,8,4096]{3,2,0,1:T(8,128)(2,1)} %copy.48), calls=%async_computation | async-start | bytes 4194304 | tf_op jit(solution)/shard_map/all_to_all | solution.py:66
  52.8 78.8 %all-gather.6.cloned.1.call-start = ((), (), s32[]{:S(2)}) async-start(), calls=%async_computation.3 | async-start | bytes 1114112 | tf_op jit(solution)/shard_map/all_gather | solution.py:93
  90.0 2.5 %copy-start.5 = (f32[8]{0:T(128)S(1)}, f32[8]{0:T(128)}, u32[]{:S(2)}) copy-start(f32[8]{0:T(128)} %param.17) | copy-start | bytes 100
  92.4 73.1 %all-gather.8.cloned.1.call-start = ((), (), s32[]{:S(2)}) async-start(), calls=%async_computation.4 | async-start | bytes 2359296 | tf_op jit(solution)/shard_map/all_gather | solution.py:123
  133.9 2.1 %copy-start.2 = (bf16[2,2048,128]{2,1,0:T(8,128)(2,1)S(1)}, bf16[2,2048,128]{2,1,0:T(8,128)(2,1)}, u32[]{:S(2)}) copy-start(bf16[2,2048,128]{2,1,0:T(8,128)(2,1)} %all-gather.6.cloned.1.call-done) | copy-start | bytes 3145732
  136.0 2.8 %copy-start.4 = (bf16[4096]{0:T(1024)(128)(2,1)S(1)}, bf16[4096]{0:T(1024)(128)(2,1)}, u32[]{:S(2)}) copy-start(bf16[4096]{0:T(1024)(128)(2,1)} %param.12) | copy-start | bytes 24580
  170.8 8.0 %copy-start.1 = (bf16[1024,512]{1,0:T(8,128)(2,1)S(1)}, bf16[1024,512]{1,0:T(8,128)(2,1)}, u32[]{:S(2)}) copy-start(bf16[1024,512]{1,0:T(8,128)(2,1)} %param.10) | copy-start | bytes 3145732
  172.3 14.8 %all-to-all-start.1 = ((bf16[2,16,8,512]{3,2,0,1:T(8,128)(2,1)}), bf16[2,16,8,512]{3,2,0,1:T(8,128)(2,1)S(1)}, u32[]{:S(2)}, u32[]{:S(2)}) async-start(bf16[2,16,8,512]{3,2,0,1:T(8,128)(2,1)} %copy.42), calls=%async_computation.1 | async-start | bytes 524288 | tf_op jit(solution)/shard_map/all_to_all | solution.py:129
Sparse Core Ops, SparseCore 0:
  13.2 29.0 all-gather.3
  92.5 38.9 all-gather.5
  139.0 26.4 all-gather.7
where the time goes:
time: 202 us
  waiting for transfers between devices  125 us (62%)
  other arithmetic  20.7 us (10%)
  matrix products  17.7 us (9%)
  between operations  15.3 us (8%)
  starting transfers between devices  13.2 us (7%)
  local copies, waits for them, and re-layouts  9.37 us (5%)
    all_gather x1, waiting for transfers between devices, on_device(): piece = lax.all_gather(paired, 'seq', axis=1, tiled=True)  34 us
    all_to_all x1, waiting for transfers between devices, on_device(): lax.all_to_all(outgoing, 'seq', split_axis=1, concat_axis=1, tiled=True)  32.2 us
    all_gather x1, waiting for transfers between devices, on_device(): whole_rows = lax.all_gather(gathered_rows, 'mp', axis=1, tiled=True)  26.6 us
    all_gather x1, waiting for transfers between devices, on_device(): lax.all_gather(attended, 'mp', axis=1, tiled=True)  26 us
    all_to_all x1, starting transfers between devices, on_device(): lax.all_to_all(outgoing, 'seq', split_axis=1, concat_axis=1, tiled=True)  6.64 us
    all_to_all x1, waiting for transfers between devices, on_device(): lax.all_to_all(outgoing_back, 'seq', split_axis=1, concat_axis=1, tiled=T...  6.56 us
    all_to_all x1, starting transfers between devices, on_device(): lax.all_to_all(outgoing_back, 'seq', split_axis=1, concat_axis=1, tiled=T...  6.52 us
    dot_general x1, matrix products, on_device(): jnp.dot(lax.all_gather(attended, 'mp', axis=1, tiled=True), final_project...  5.31 us
  transfers between devices with their start and end apart: 5, of which 5 were waited for; matrix products, arithmetic and copies ran while one was open for 4% of the time, Pallas kernels for 0%

commit v1 on v0

--- a/solution.py
+++ b/solution.py
@@ -90,7 +90,9 @@
         own_slots // block_rows * nseq * block_rows + shard * block_rows + own_slots % block_rows
     )
     start_best = jnp.full((memory_pair_portion, asker_cluster, owned), -1e30, jnp.float32)
-    piece = lax.all_gather(paired, "seq", axis=1, tiled=True)
+    piece = jnp.concatenate(
+        lax.all_to_all(jnp.stack([paired] * lax.axis_size("seq")), "seq", 0, 0), axis=1
+    )
     best = start_best
     count = piece.shape[1]
     key_piece = piece[0].reshape(count, memory_pair_portion, PER_HEAD_DIM)

time: 202 us -> 180 us (0.89)
  waiting for transfers between devices: 125 us -> 98.6 us
  starting transfers between devices: 13.2 us -> 17 us
  local copies, waits for them, and re-layouts: 9.37 us -> 11.8 us
    all_gather x1 -> x0, waiting for transfers between devices: 34 us -> none  [on_device(): piece = lax.all_gather(paired, 'seq', axis=1, tiled=True)]
    all_to_all x0 -> x1, waiting for transfers between devices: none -> 9.57 us  [on_device(): lax.all_to_all(jnp.stack([paired] * lax.axis_size('seq')), 'seq', 0, 0)]
    all_to_all x0 -> x1, starting transfers between devices: none -> 3.66 us  [on_device(): lax.all_to_all(jnp.stack([paired] * lax.axis_size('seq')), 'seq', 0, 0)]
    all_gather x1, waiting for transfers between devices: 26 us -> 23.6 us  [on_device(): lax.all_gather(attended, 'mp', axis=1, tiled=True)]
  transfers between devices with their start and end apart: 5 -> 5, of which waited for: 5 -> 5; matrix products, arithmetic and copies ran while one was open for 4% -> 5% of each run, Pallas kernels for 0% -> 0%
where the time goes in v1:
time: 180 us; the launch traced here: 179 us
  waiting for transfers between devices  98.6 us (55%)
  other arithmetic  20 us (11%)
  starting transfers between devices  17 us (9%)
  matrix products  16.2 us (9%)
  between operations  15.6 us (9%)
  local copies, waits for them, and re-layouts  11.8 us (7%)
    all_to_all x1, waiting for transfers between devices, on_device(): lax.all_to_all(outgoing, 'seq', split_axis=1, concat_axis=1, tiled=True)  32.1 us
    all_gather x1, waiting for transfers between devices, on_device(): whole_rows = lax.all_gather(gathered_rows, 'mp', axis=1, tiled=True)  26.6 us
    all_gather x1, waiting for transfers between devices, on_device(): lax.all_gather(attended, 'mp', axis=1, tiled=True)  23.6 us
    all_to_all x1, waiting for transfers between devices, on_device(): lax.all_to_all(jnp.stack([paired] * lax.axis_size('seq')), 'seq', 0, 0)  9.57 us
    all_to_all x1, starting transfers between devices, on_device(): lax.all_to_all(outgoing, 'seq', split_axis=1, concat_axis=1, tiled=True)  6.64 us
    all_to_all x1, waiting for transfers between devices, on_device(): lax.all_to_all(outgoing_back, 'seq', split_axis=1, concat_axis=1, tiled=T...  6.57 us
    all_to_all x1, starting transfers between devices, on_device(): lax.all_to_all(outgoing_back, 'seq', split_axis=1, concat_axis=1, tiled=T...  6.53 us
    dot_general x1, matrix products, on_device(): jnp.dot(normed, asker_projection, preferred_element_type=jnp.float32)  5.39 us
  transfers between devices with their start and end apart: 5, of which 5 were waited for; matrix products, arithmetic and copies ran while one was open for 5% of the time, Pallas kernels for 0%

profile of v1, /device:TPU:1, one launch (start us, length us, event | category | flops | bytes accessed | tf_op | source)
XLA Modules:
  0.0 179.3 jit_solution(14133165608141298193)
XLA Ops:
  6.5 0.9 reduce_sum.69
  7.7 0.6 and_select_fusion.4
  8.3 0.6 iota_compare_fusion.1
  9.0 0.7 compare_select_fusion
  9.7 2.6 %gather_fusion = bf16[256,512]{1,0:T(8,128)(2,1)S(1)} fusion(bf16[1024,512]{1,0:T(8,128)(2,1)} %param.10, s32[1024]{0:T(1024)S(1)} %pad_clamp_fusion.2), kind=kCustom, calls=%fused_computation | custom fusion | bytes 525312 | tf_op jit(solution)/shard_map/gather | solution.py:60
  12.3 0.8 broadcast_select_fusion
  13.1 0.6 fusion.52
  15.6 26.6 %all-gather.3.cloned.1.call-done = bf16[256,4096]{1,0:T(8,128)(2,1)} async-done(((bf16[256,512]{1,0:T(8,128)(2,1)}), bf16[256,4096]{1,0:T(8,128)(2,1)}) %all-gather.3.cloned.1.call-update) | async-done | bytes 2097168 | tf_op jit(solution)/shard_map/all_gather | solution.py:62
  42.3 2.4 %fusion.7 = bf16[2,16,8,4096]{3,2,1,0:T(8,128)(2,1)S(1)} fusion(s32[]{:T(128)S(6)} %select_n.208, bf16[2,16,8,4096]{3,2,1,0:T(8,128)(2,1)} %bitcast.124), kind=kLoop, calls=%fused_computation.15 | loop fusion | flops 1048576 | bytes 4194308 | tf_op jit(solution)/shard_map/jit(_roll_dynamic)/concatenate | solution.py:63
  44.6 1.5 copy.47
  46.1 6.6 %all-to-all-start = ((bf16[2,16,8,4096]{3,2,0,1:T(8,128)(2,1)}), bf16[2,16,8,4096]{3,2,0,1:T(8,128)(2,1)S(1)}, u32[]{:S(2)}, u32[]{:S(2)}) async-start(bf16[2,16,8,4096]{3,2,0,1:T(8,128)(2,1)} %copy.47), calls=%async_computation | async-start | bytes 4194304 | tf_op jit(solution)/shard_map/all_to_all | solution.py:66
  53.2 32.1 %all-to-all-done = bf16[2,16,8,4096]{3,2,0,1:T(8,128)(2,1)S(1)} async-done(((bf16[2,16,8,4096]{3,2,0,1:T(8,128)(2,1)}), bf16[2,16,8,4096]{3,2,0,1:T(8,128)(2,1)S(1)}, u32[]{:S(2)}, u32[]{:S(2)}) %all-to-all-start) | async-done | bytes 2097184 | tf_op jit(solution)/shard_map/all_to_all | solution.py:66
  85.4 1.5 copy.38
  86.9 2.2 %gather_fusion.1 = bf16[16,8,4096]{2,1,0:T(8,128)(2,1)S(1)} fusion(bf16[32,8,4096]{2,1,0:T(8,128)(2,1)} %bitcast.122, s32[1024]{0:T(1024)S(1)} %pad_clamp_fusion.1), kind=kCustom, calls=%fused_computation.1 | custom fusion | bytes 2097216 | tf_op jit(solution)/shard_map/gather | solution.py:22
  89.5 0.5 fusion.11
  90.8 1.2 stack.11
  92.0 3.7 %all-to-all-start.1 = ((bf16[16,2,128,128]{3,2,1,0:T(8,128)(2,1)}), bf16[16,2,128,128]{3,2,1,0:T(8,128)(2,1)S(1)}, u32[]{:S(2)}, u32[]{:S(2)}) async-start(bf16[16,2,128,128]{3,2,1,0:T(8,128)(2,1)} %stack.11), calls=%async_computation.1 | async-start | bytes 2097152 | tf_op jit(solution)/shard_map/all_to_all | solution.py:94
  96.3 5.4 %fusion.8 = bf16[16,8,8,128]{3,2,1,0:T(8,128)(2,1)} fusion(bf16[4096,1024]{1,0:T(8,128)(2,1)} %param.13, bf16[16,8,4096]{2,1,0:T(8,128)(2,1)S(1)} %gather_fusion.1, f32[4096]{0:T(1024)S(1)} %convert_element_type.49, f32[128]{0:T(128)S(1)} %rsqrt.12), kind=kOutput, calls=%fused_computation.20 | convolution fusion | flops 1075970048 | bytes 9716224 | tf_op jit(solution)/shard_map/dot_general | solution.py:72
  101.7 9.6 %all-to-all-done.1 = bf16[16,2,128,128]{3,2,1,0:T(8,128)(2,1)S(1)} async-done(((bf16[16,2,128,128]{3,2,1,0:T(8,128)(2,1)}), bf16[16,2,128,128]{3,2,1,0:T(8,128)(2,1)S(1)}, u32[]{:S(2)}, u32[]{:S(2)}) %all-to-all-start.1) | async-done | bytes 1048608 | tf_op jit(solution)/shard_map/all_to_all | solution.py:94
  111.3 0.9 copy-done.2
  112.2 1.3 fusion
  113.5 2.1 %fusion.1 = f32[8,128]{1,0:T(8,128)S(1)} fusion(f32[2048,128,8]{1,0,2:T(8,128)S(1)} %get-tuple-element.12, f32[8,128]{1,0:T(8,128)S(1)} %broadcast_maximum_fusion, f32[8]{0:T(128)S(1)} %broadcast_multiply_fusion, pred[128,2048]{0,1:T(8,128)(4,1)S(1)} %broadcast_compare_fusion), kind=kLoop, calls=%fused_computation.8 | loop fusion | flops 10484736 | bytes 8658976 | tf_op jit(solution)/shard_map/reduce_sum | solution.py:111
  115.6 2.9 %fusion.21 = bf16[8,128,128]{1,2,0:T(8,128)(2,1)} fusion(bf16[2048,128,1]{1,0,2:T(8,128)(2,1)S(1)} %bitcast.127, f32[2048,128,8]{1,0,2:T(8,128)S(1)} %get-tuple-element.12, f32[8,128]{1,0:T(8,128)S(1)} %broadcast_maximum_fusion, f32[8]{0:T(128)S(1)} %broadcast_multiply_fusion, pred[128,2048]{0,1:T(8,128)(4,1)S(1)} %broadcast_compare_fusion, ...), kind=kOutput, calls=%fused_computation.34 | convolution fusion | flops 547618816 | bytes 9445408 | tf_op jit(solution)/shard_map/ngqk,knd->ngqd/dot_general | solution.py:112
  119.2 23.6 %all-gather.5.cloned.1.call-done = bf16[128,8192]{0,1:T(8,128)(2,1)} async-done(((bf16[128,1024]{0,1:T(8,128)(2,1)}), bf16[128,8192]{0,1:T(8,128)(2,1)}) %all-gather.5.cloned.1.call-update) | async-done | bytes 2097168 | tf_op jit(solution)/shard_map/all_gather | solution.py:125
  142.8 5.3 %fusion.10 = bf16[16,8,512]{2,1,0:T(8,128)(2,1)S(1)} fusion(bf16[128,8192]{0,1:T(8,128)(2,1)} %all-gather.5.cloned.1.call-done, bf16[8192,512]{1,0:T(8,128)(2,1)} %param.16, f32[128]{0:T(128)S(1)} %fusion.16), kind=kOutput, calls=%fused_computation.22 | convolution fusion | flops 1073872896 | bytes 10617344 | tf_op jit(solution)/shard_map/dot_general | solution.py:124
  148.2 0.6 gather_fusion.2
  148.8 0.7 copy.42
  149.6 6.5 %all-to-all-start.2 = ((bf16[2,16,8,512]{3,2,0,1:T(8,128)(2,1)}), bf16[2,16,8,512]{3,2,0,1:T(8,128)(2,1)S(1)}, u32[]{:S(2)}, u32[]{:S(2)}) async-start(bf16[2,16,8,512]{3,2,0,1:T(8,128)(2,1)} %copy.42), calls=%async_computation.2 | async-start | bytes 524288 | tf_op jit(solution)/shard_map/all_to_all | solution.py:131
  156.1 1.6 convert_element_type.45
  157.8 6.6 %all-to-all-done.2 = bf16[2,16,8,512]{3,2,0,1:T(8,128)(2,1)S(1)} async-done(((bf16[2,16,8,512]{3,2,0,1:T(8,128)(2,1)}), bf16[2,16,8,512]{3,2,0,1:T(8,128)(2,1)S(1)}, u32[]{:S(2)}, u32[]{:S(2)}) %all-to-all-start.2) | async-done | bytes 262176 | tf_op jit(solution)/shard_map/all_to_all | solution.py:131
  164.6 5.2 %scatter_custom_fusion = f32[1024,512]{1,0:T(8,128)} fusion(f32[1024,512]{1,0:T(8,128)} %convert_element_type.45, s32[256]{0:T(256)S(1)} %bitcast.130, bf16[256,512]{1,0:T(8,128)(2,1)S(1)} %bitcast_select_fusion.1), kind=kCustom, calls=%fused_computation.37 | custom fusion | flops 262144 | bytes 2359296 | tf_op jit(solution)/shard_map/scatter-add | solution.py:135
  169.8 2.7 %convert_element_type.59 = bf16[1024,512]{1,0:T(8,128)(2,1)} convert(f32[1024,512]{1,0:T(8,128)} %scatter_custom_fusion) | non-fusion elementwise | flops 524288 | bytes 3145728 | tf_op jit(solution)/shard_map/convert_element_type | solution.py:137
  (49 shorter events, 3.6 us)
Async XLA Ops:
  6.5 83.0 %copy-start = (bf16[4096,128]{1,0:T(8,128)(2,1)S(1)}, bf16[4096,128]{1,0:T(8,128)(2,1)}, u32[]{:S(2)}) copy-start(bf16[4096,128]{1,0:T(8,128)(2,1)} %param.14) | copy-start | bytes 3145732
  6.5 35.7 %all-gather.3.cloned.1.call-start = ((), (), s32[]{:S(2)}) async-start(), calls=%async_computation.3 | async-start | bytes 2359296 | tf_op jit(solution)/shard_map/all_gather | solution.py:62
  46.1 6.7 %copy-start.3 = (bf16[4096]{0:T(1024)(128)(2,1)S(1)}, bf16[4096]{0:T(1024)(128)(2,1)}, u32[]{:S(2)}) copy-start(bf16[4096]{0:T(1024)(128)(2,1)} %param.11) | copy-start | bytes 24580
  46.1 7.1 %copy-start.6 = (f32[8]{0:T(128)S(1)}, f32[8]{0:T(128)}, u32[]{:S(2)}) copy-start(f32[8]{0:T(128)} %param.17) | copy-start | bytes 100
  46.1 39.3 %all-to-all-start = ((bf16[2,16,8,4096]{3,2,0,1:T(8,128)(2,1)}), bf16[2,16,8,4096]{3,2,0,1:T(8,128)(2,1)S(1)}, u32[]{:S(2)}, u32[]{:S(2)}) async-start(bf16[2,16,8,4096]{3,2,0,1:T(8,128)(2,1)} %copy.47), calls=%async_computation | async-start | bytes 4194304 | tf_op jit(solution)/shard_map/all_to_all | solution.py:66
  89.1 1.2 copy-start.5
  92.0 19.2 %all-to-all-start.1 = ((bf16[16,2,128,128]{3,2,1,0:T(8,128)(2,1)}), bf16[16,2,128,128]{3,2,1,0:T(8,128)(2,1)S(1)}, u32[]{:S(2)}, u32[]{:S(2)}) async-start(bf16[16,2,128,128]{3,2,1,0:T(8,128)(2,1)} %stack.11), calls=%async_computation.1 | async-start | bytes 2097152 | tf_op jit(solution)/shard_map/all_to_all | solution.py:94
  95.7 47.1 %all-gather.5.cloned.1.call-start = ((), (), s32[]{:S(2)}) async-start(), calls=%async_computation.4 | async-start | bytes 2359296 | tf_op jit(solution)/shard_map/all_gather | solution.py:125
  111.2 1.0 copy-start.2
  115.6 2.9 %copy-start.4 = (bf16[4096]{0:T(1024)(128)(2,1)S(1)}, bf16[4096]{0:T(1024)(128)(2,1)}, u32[]{:S(2)}) copy-start(bf16[4096]{0:T(1024)(128)(2,1)} %param.12) | copy-start | bytes 24580
  148.1 8.0 %copy-start.1 = (bf16[1024,512]{1,0:T(8,128)(2,1)S(1)}, bf16[1024,512]{1,0:T(8,128)(2,1)}, u32[]{:S(2)}) copy-start(bf16[1024,512]{1,0:T(8,128)(2,1)} %param.10) | copy-start | bytes 3145732
  149.6 14.8 %all-to-all-start.2 = ((bf16[2,16,8,512]{3,2,0,1:T(8,128)(2,1)}), bf16[2,16,8,512]{3,2,0,1:T(8,128)(2,1)S(1)}, u32[]{:S(2)}, u32[]{:S(2)}) async-start(bf16[2,16,8,512]{3,2,0,1:T(8,128)(2,1)} %copy.42), calls=%async_computation.2 | async-start | bytes 524288 | tf_op jit(solution)/shard_map/all_to_all | solution.py:131
Sparse Core Ops, SparseCore 0:
  13.2 29.0 all-gather.2
  118.6 24.1 all-gather.4
